TPU v7x, 128 devices: a whole 4x4x4 slice. The times are simulated.
128 devices in a mesh: frames: 64 (over z, y, x_lo, core), dp: 2 (over x_hi).
Axes of the slice: x: 4 (x_hi: 2, x_lo: 2; x = x_hi * 2 + x_lo), y: 4, z: 4, core: 2. Of those that a mesh axis runs over, the one named last changes fastest.
Arguments:
- shifted: bfloat16 [2, 256, 16, 16, 640], P('dp', 'frames'), may hold values from -6 to 6
- out_grad: bfloat16 [2, 256, 16, 16, 640], P('dp', 'frames'), may hold values from -6 to 6
- conv_weight: bfloat16 [640, 5760], P('frames'), may hold values from -0.078125 to 0.078125
- norm_gain: float32 [640], replicated, may hold values from 0.5 to 2
- norm_bias: float32 [640], replicated, may hold values from -4 to 4
- shift_fwd: int32 [80], replicated, may hold values from 0 to 639, as said below
- shift_bwd: int32 [80], replicated, may hold values from 0 to 639, as said below
Outputs:
- in_grad: bfloat16 [2, 256, 16, 16, 640], P('dp', 'frames')
- weight_grad: float32 [640, 5760], P('frames')
- gain_grad: float32 [640], replicated
- bias_grad: float32 [640], replicated
Inputs may be any that keep to these rules, and one draw needn't show every extreme that they name: `shift_fwd`: 80 distinct channel numbers, none of them in shift_bwd. `shift_bwd`: 80 distinct channel numbers, none of them in shift_fwd.
All inputs are finite; a program needn't handle non-finite values.
Results may differ from a plain program's by a relative error of at most 0.003.
Values may be sent and summed in bfloat16 or wider, within the bound.
A program may use at most 128 MiB of HBM per device.

v0:
```python
import jax
import jax.numpy as jnp
from jax import lax
from jax.sharding import PartitionSpec as P

GROUP_CH = 20
epsilon = 1e-05


def with_halo(x, sides, width):
    for axis, dim in sides:
        size, length = (lax.axis_size(axis), x.shape[dim])
        up = [(i, (i + 1) % size) for i in range(size - 1)]
        down = [(j, i) for i, j in up]
        last = lax.slice_in_dim(x, length - width, length, axis=dim)
        first = lax.slice_in_dim(x, 0, width, axis=dim)
        before = lax.ppermute(last, axis, up)
        after = lax.ppermute(first, axis, down)
        x = jnp.concatenate([before, x, after], axis=dim)
    return x


def pad_space(values):
    return jnp.pad(values, ((0, 0), (1, 1), (1, 1), (0, 0)))


def on_device(shifted, out_grad, conv_weight, norm_gain, norm_bias, shift_fwd, shift_bwd):
    frames_local = shifted[0]
    grad_local = out_grad[0]
    frame_count, row_count, col_count, channels = frames_local.shape
    groups = channels // GROUP_CH
    whole_weight = lax.all_gather(conv_weight, "frames", axis=0, tiled=True)
    values = frames_local.astype(jnp.float32).reshape(
        frame_count, row_count * col_count, groups, GROUP_CH
    )
    center = jnp.mean(values, axis=(1, 3), keepdims=True)
    spread = jnp.mean(jnp.square(values - center), axis=(1, 3), keepdims=True)
    inverse = lax.rsqrt(spread + epsilon)
    grouped_normed = (values - center) * inverse
    normed = grouped_normed.reshape(frame_count, row_count, col_count, channels)
    before = normed * norm_gain + norm_bias
    activation = jax.nn.silu(before).astype(jnp.bfloat16)
    act_padded = pad_space(activation)
    grad_padded = pad_space(grad_local)
    grad_rows = grad_local.reshape(-1, channels)
    act_grad = jnp.zeros((grad_rows.shape[0], channels), jnp.float32)
    for tap_index in range(9):
        row_off, col_off = divmod(tap_index, 3)
        grad_view = grad_padded[
            :, 2 - row_off : 2 - row_off + row_count, 2 - col_off : 2 - col_off + col_count, :
        ].reshape(-1, channels)
        act_grad = act_grad + jnp.dot(
            grad_view,
            whole_weight[:, tap_index * channels : (tap_index + 1) * channels],
            preferred_element_type=jnp.float32,
        )
    scale = float(
        lax.axis_size("dp") * lax.axis_size("frames") * frame_count * row_count * col_count
    ) ** (-0.5)
    parts = []
    for tap_index in range(9):
        row_off, col_off = divmod(tap_index, 3)
        act_view = act_padded[
            :, row_off : row_off + row_count, col_off : col_off + col_count, :
        ].reshape(-1, channels)
        parts.append(
            lax.dot_general(
                grad_rows, act_view, (((0,), (0,)), ((), ())), preferred_element_type=jnp.float32
            )
        )
    kernel_shard = lax.psum_scatter(
        jnp.concatenate(parts, axis=1), "frames", scatter_dimension=0, tiled=True
    )
    kernel_shard = lax.psum(kernel_shard, "dp")
    weight_grad = kernel_shard * scale
    sigmoid_val = jax.nn.sigmoid(before)
    pre_grad = act_grad.reshape(before.shape) * sigmoid_val * (1.0 + before * (1.0 - sigmoid_val))
    gain_part = jnp.sum(pre_grad * normed, axis=(0, 1, 2))
    bias_part = jnp.sum(pre_grad, axis=(0, 1, 2))
    gain_total, bias_total = lax.psum((gain_part, bias_part), ("frames", "dp"))
    norm_grad = (pre_grad * norm_gain).reshape(values.shape)
    first_mean = jnp.mean(norm_grad, axis=(1, 3), keepdims=True)
    second_mean = jnp.mean(norm_grad * grouped_normed, axis=(1, 3), keepdims=True)
    shifted_grad = (
        ((norm_grad - first_mean - grouped_normed * second_mean) * inverse)
        .reshape(frames_local.shape)
        .astype(jnp.bfloat16)
    )
    channel_ids = jnp.arange(channels, dtype=jnp.int32)
    forward_match = channel_ids[None, :] == shift_fwd[:, None]
    backward_match = channel_ids[None, :] == shift_bwd[:, None]
    forward_select = forward_match.astype(jnp.bfloat16)
    backward_select = backward_match.astype(jnp.bfloat16)
    forward_mask = jnp.any(forward_match, axis=0)
    backward_mask = jnp.any(backward_match, axis=0)
    plane = row_count * col_count
    first_frame = shifted_grad[0].reshape(plane, channels)
    last_frame = shifted_grad[frame_count - 1].reshape(plane, channels)
    contract_channels = (((1,), (1,)), ((), ()))
    rim_first = lax.dot_general(
        forward_select, first_frame, contract_channels, preferred_element_type=jnp.float32
    ).astype(jnp.bfloat16)
    rim_last = lax.dot_general(
        backward_select, last_frame, contract_channels, preferred_element_type=jnp.float32
    ).astype(jnp.bfloat16)
    extended = with_halo(jnp.stack([rim_first, rim_last]), (("frames", 0),), 1)
    contract_fold = (((0,), (0,)), ((), ()))
    from_prev = lax.dot_general(
        extended[0], backward_select, contract_fold, preferred_element_type=jnp.float32
    ).astype(jnp.bfloat16)
    from_next = lax.dot_general(
        extended[3], forward_select, contract_fold, preferred_element_type=jnp.float32
    ).astype(jnp.bfloat16)
    from_prev = from_prev.reshape(1, row_count, col_count, channels)
    from_next = from_next.reshape(1, row_count, col_count, channels)
    later = jnp.concatenate([shifted_grad[1:], from_next], axis=0)
    earlier = jnp.concatenate([from_prev, shifted_grad[:-1]], axis=0)
    in_grad = jnp.where(forward_mask, later, jnp.where(backward_mask, earlier, shifted_grad))
    return (in_grad[None], weight_grad, gain_total * scale, bias_total * scale)


def solution(mesh):
    in_specs = (
        P("dp", "frames", None, None, None),
        P("dp", "frames", None, None, None),
        P("frames", None),
        P(),
        P(),
        P(),
        P(),
    )
    out_specs = (P("dp", "frames", None, None, None), P("frames", None), P(), P())
    return jax.shard_map(
        on_device, mesh=mesh, in_specs=in_specs, out_specs=out_specs, check_vma=False
    )
```

profile of v0, /device:TPU:1, one launch (start us, length us, event | category | flops | bytes accessed | tf_op | source)
XLA Modules:
  0.0 923.6 jit_solution(15676079137542957894)
XLA Ops:
  8.0 21.9 %reshape.226 = f32[4,256,32,20]{3,2,1,0:T(8,128)} reshape(bf16[1,4,16,16,640]{4,3,2,1,0:T(8,128)(2,1)} %param.7) | data formatting | bytes 3932160 | tf_op jit(solution)/shard_map/convert_element_type | solution.py:33
  31.5 11.5 %copy.33 = f32[4,256,32,20]{1,0,3,2:T(4,128)} copy(f32[4,256,32,20]{3,2,1,0:T(8,128)} %reshape.226) | data formatting | bytes 5242880 | tf_op jit(solution)/shard_map/convert_element_type | solution.py:33
  43.2 8.8 pad_slice_fusion.8
  52.0 78.7 %all-gather.3.cloned.1.call-done = bf16[64,10,5760]{2,1,0:T(8,128)(2,1)} async-done(((bf16[1,10,5760]{2,1,0:T(8,128)(2,1)}), bf16[64,10,5760]{2,1,0:T(8,128)(2,1)}) %all-gather.3.cloned.1.call-update) | async-done | bytes 7372816 | tf_op jit(solution)/shard_map/all_gather | solution.py:32
  130.7 13.8 %reshape.229 = bf16[640,5760]{1,0:T(8,128)(2,1)} reshape(bf16[64,10,5760]{2,1,0:T(8,128)(2,1)} %all-gather.3.cloned.1.call-done) | data formatting | bytes 14745600
  144.6 3.0 fusion.4
  155.3 2.8 fusion.18
  158.1 2.8 fusion.16
  160.9 6.2 fusion.28
  167.1 3.3 copy.31
  170.3 4.2 reshape.215
  174.5 16.5 %fusion.29 = (f32[4,32]{0,1:T(8,128)S(1)}, f32[4,32]{0,1:T(8,128)S(1)}) fusion(f32[4,32]{0,1:T(8,128)S(1)} %copy.34, f32[4,256,32,20]{1,0,3,2:T(4,128)} %copy.33, f32[4,32]{0,1:T(8,128)S(1)} %copy.32, f32[4,256,32,20]{1,0,3,2:T(4,128)} %reshape.215, f32[32,20]{1,0:T(8,128)S(1)} %add.134, f32[32,20]{1,0:T(8,128)S(1)} %mul.201), kind=kLoop, calls=%fused_computation.88 | loop fusion | flops 10485504 | bytes 5250048 | tf_op jit(solution)/shard_map/reduce_sum | solution.py:82
  191.6 3.6 multiply_convert_fusion
  195.2 3.0 pad_slice_fusion
  207.9 2.4 bitcast_dynamic-update-slice_fusion.4
  212.7 2.5 bitcast_dynamic-update-slice_fusion.2
  224.9 3.4 collective-permute-start.1
  228.2 67.9 %all-reduce.3 = (f32[640]{0:T(1024)S(1)}, f32[640]{0:T(1024)S(1)}) all-reduce(f32[640]{0:T(1024)S(1)} %get-tuple-element.25, f32[640]{0:T(1024)S(1)} %get-tuple-element.24), channel_id=1, replica_groups=mesh['frames'=64,'dp'=2] {'frames','dp'}, use_global_device_ids=true, to_apply=%region_11.12 | all-reduce | flops 1280 | bytes 10240 | tf_op jit(solution)/shard_map/psum | solution.py:80
  300.3 516.5 %all-reduce.9.cloned.1.call-done = f32[640,5760]{0,1:T(8,128)} async-done(((f32[640,5760]{0,1:T(8,128)}), f32[640,5760]{0,1:T(8,128)}) %all-reduce.9.cloned.1.call-update) | async-done | bytes 14745616
  816.7 5.1 constant_dynamic-slice_fusion
  823.3 4.4 maximum_select_fusion
  827.7 82.4 %all-reduce.7.cloned.1.call-done = f32[10,5760]{0,1:T(8,128)} async-done(((f32[10,5760]{0,1:T(8,128)}), f32[10,5760]{0,1:T(8,128)}) %all-reduce.7.cloned.1.call-update) | async-done | bytes 230416 | tf_op jit(solution)/shard_map/psum | solution.py:74
  910.1 3.7 broadcast_multiply_fusion
  913.8 3.0 copy.37
  (88 shorter events, 37.4 us)
Async XLA Ops:
  7.2 123.5 %all-gather.3.cloned.1.call-start = ((), (), s32[]{:S(2)}) async-start(), calls=%async_computation.1 | async-start | bytes 11980800 | tf_op jit(solution)/shard_map/all_gather | solution.py:32
  7.9 22.0 %copy-start = (bf16[1,4,16,16,640]{4,3,2,1,0:T(8,128)(2,1)S(1)}, bf16[1,4,16,16,640]{4,3,2,1,0:T(8,128)(2,1)}, u32[]{:S(2)}) copy-start(bf16[1,4,16,16,640]{4,3,2,1,0:T(8,128)(2,1)} %param.7) | copy-start | bytes 3932164
  7.9 808.8 %all-reduce.9.cloned.1.call-start = ((), (), s32[]{:S(2)}) async-start(), calls=%async_computation.2 | async-start | bytes 29491200
  31.5 11.5 %copy-start.12 = (f32[640]{0:T(1024)S(1)}, f32[640]{0:T(1024)}, u32[]{:S(2)}) copy-start(f32[640]{0:T(1024)} %param.11) | copy-start | bytes 7684
  31.5 11.6 %copy-start.13 = (f32[640]{0:T(1024)S(1)}, f32[640]{0:T(1024)}, u32[]{:S(2)}) copy-start(f32[640]{0:T(1024)} %param.10) | copy-start | bytes 7684
  144.5 3.7 copy-start.1
  144.6 4.0 copy-start.11
  148.6 1.3 copy-start.10
  149.9 1.3 copy-start.4
  151.3 1.3 copy-start.9
  152.6 1.3 copy-start.8
  154.0 1.3 copy-start.7
  155.3 2.8 copy-start.6
  195.2 3.0 copy-start.5
  220.1 0.7 copy-start.16
  220.1 1.9 copy-start.14
  220.1 1.9 copy-start.15
  220.1 690.0 %all-reduce.7.cloned.1.call-start = ((), (), s32[]{:S(2)}) async-start(), calls=%async_computation | async-start | bytes 5898240 | tf_op jit(solution)/shard_map/psum | solution.py:74
  222.4 75.8 %collective-permute-start = (bf16[1,80,256]{2,1,0:T(8,128)(2,1)S(1)}, bf16[1,80,256]{2,1,0:T(8,128)(2,1)S(1)}, u32[]{:S(2)}, u32[]{:S(2)}) collective-permute-start(bf16[1,80,256]{2,1,0:T(8,128)(2,1)S(1)} %fusion.1), channel_id=1, source_target_pairs={{2,0},{4,2},{6,4},{8,6},{10,8},{12,10},{14,12},{16,14},{18,16},{20... | collective-permute-start | bytes 122888 | tf_op jit(solution)/shard_map/ppermute | solution.py:18
  224.9 74.4 %collective-permute-start.1 = (bf16[1,80,256]{2,1,0:T(8,128)(2,1)S(1)}, bf16[1,80,256]{2,1,0:T(8,128)(2,1)S(1)}, u32[]{:S(2)}, u32[]{:S(2)}) collective-permute-start(bf16[1,80,256]{2,1,0:T(8,128)(2,1)S(1)} %fusion.2), channel_id=1, source_target_pairs={{0,2},{2,4},{4,6},{6,8},{8,10},{10,12},{12,14},{14,16},{16,18},{18... | collective-permute-start | bytes 122888 | tf_op jit(solution)/shard_map/ppermute | solution.py:17
  821.8 1.2 copy-start.2
  821.8 1.5 copy-start.3
Sparse Core Ops, SparseCore 0:
  9.7 120.9 all-gather.2
  220.2 596.4 all-reduce.8
  822.0 88.0 all-reduce.6
where the time goes:
time: 929 us; the launch traced here: 924 us
  waiting for transfers between devices  678 us (73%)
  local copies, waits for them, and re-layouts  81.4 us (9%)
  blocking collectives  67.9 us (7%)
  matrix products  45.7 us (5%)
  other arithmetic  29.7 us (3%)
  between operations  15 us (2%)
    unnamed x4, waiting for transfers between devices  517 us
    psum x1, waiting for transfers between devices, on_device(): kernel_shard = lax.psum(kernel_shard, 'dp')  82.4 us
    all_gather x1, waiting for transfers between devices, on_device(): whole_weight = lax.all_gather(conv_weight, 'frames', axis=0, tiled=True)  78.7 us
    psum x1, blocking collectives, on_device(): gain_total, bias_total = lax.psum((gain_part, bias_part), ('frames', 'dp'))  67.9 us
    convert_element_type x2, local copies, waits for them, and re-layouts, on_device(): frames_local.astype(jnp.float32)  33.4 us
    unnamed x38, local copies, waits for them, and re-layouts  25.6 us
    dot_general x9, matrix products, on_device(): lax.dot_general(grad_rows, act_view, (((0,), (0,)), ((), ())), preferred_...  21.8 us
    dot_general x9, matrix products, on_device(): jnp.dot(grad_view, whole_weight[:, tap_index * channels:(tap_index + 1) *...  21.3 us
  transfers between devices with their start and end apart: 5, of which 3 were waited for; matrix products, arithmetic and copies ran while one was open for 6% of the time, Pallas kernels for 0%

commit v1 on v0

--- a/solution.py
+++ b/solution.py
@@ -29,7 +29,9 @@
     grad_local = out_grad[0]
     frame_count, row_count, col_count, channels = frames_local.shape
     groups = channels // GROUP_CH
-    whole_weight = lax.all_gather(conv_weight, "frames", axis=0, tiled=True)
+    whole_weight = jnp.concatenate(
+        lax.all_to_all(jnp.stack([conv_weight] * lax.axis_size("frames")), "frames", 0, 0), axis=0
+    )
     values = frames_local.astype(jnp.float32).reshape(
         frame_count, row_count * col_count, groups, GROUP_CH
     )

time: 929 us -> 999 us (1.075)
  starting transfers between devices: 5.68 us -> 37.5 us
  waiting for transfers between devices: 678 us -> 709 us
    all_to_all x0 -> x1, waiting for transfers between devices: none -> 109 us  [on_device(): lax.all_to_all(jnp.stack([conv_weight] * lax.axis_size('frames')), 'frame...]
    all_gather x1 -> x0, waiting for transfers between devices: 78.7 us -> none  [on_device(): whole_weight = lax.all_gather(conv_weight, 'frames', axis=0, tiled=True)]
    ppermute x1, starting transfers between devices: 3.38 us -> 23.5 us  [with_halo(): before = lax.ppermute(last, axis, up)]
    reshape x0 -> x1, local copies, waits for them, and re-layouts: none -> 13.8 us  [on_device(): jnp.concatenate(lax.all_to_all(jnp.stack([conv_weight] * lax.axis_size('f...]
    unnamed x38 -> x37, local copies, waits for them, and re-layouts: 25.6 us -> 11.8 us
    all_to_all x0 -> x1, starting transfers between devices: none -> 11.2 us  [on_device(): lax.all_to_all(jnp.stack([conv_weight] * lax.axis_size('frames')), 'frame...]
    unnamed x4 -> x3, waiting for transfers between devices: 517 us -> 518 us
  transfers between devices with their start and end apart: 5 -> 5, of which waited for: 3 -> 3; matrix products, arithmetic and copies ran while one was open for 6% -> 5% of each run, Pallas kernels for 0% -> 0%
where the time goes in v1:
time: 999 us; the launch traced here: 992 us
  waiting for transfers between devices  709 us (71%)
  local copies, waits for them, and re-layouts  85.5 us (9%)
  blocking collectives  69.7 us (7%)
  matrix products  45.7 us (5%)
  starting transfers between devices  37.5 us (4%)
  other arithmetic  29.7 us (3%)
  between operations  15.3 us (2%)
    unnamed x3, waiting for transfers between devices  518 us
    all_to_all x1, waiting for transfers between devices, on_device(): lax.all_to_all(jnp.stack([conv_weight] * lax.axis_size('frames')), 'frame...  109 us
    psum x1, waiting for transfers between devices, on_device(): kernel_shard = lax.psum(kernel_shard, 'dp')  82.4 us
    psum x1, blocking collectives, on_device(): gain_total, bias_total = lax.psum((gain_part, bias_part), ('frames', 'dp'))  69.7 us
    convert_element_type x2, local copies, waits for them, and re-layouts, on_device(): frames_local.astype(jnp.float32)  32 us
    ppermute x1, starting transfers between devices, with_halo(): before = lax.ppermute(last, axis, up)  23.5 us
    dot_general x9, matrix products, on_device(): lax.dot_general(grad_rows, act_view, (((0,), (0,)), ((), ())), preferred_...  21.8 us
    dot_general x9, matrix products, on_device(): jnp.dot(grad_view, whole_weight[:, tap_index * channels:(tap_index + 1) *...  21.4 us
  transfers between devices with their start and end apart: 5, of which 3 were waited for; matrix products, arithmetic and copies ran while one was open for 5% of the time, Pallas kernels for 0%

profile of v1, /device:TPU:1, one launch (start us, length us, event | category | flops | bytes accessed | tf_op | source)
XLA Modules:
  0.0 992.5 jit_solution(17211687461772730011)
XLA Ops:
  7.2 6.0 stack.6
  13.1 11.2 %all-to-all-start = ((bf16[64,10,5760]{2,1,0:T(8,128)(2,1)}), bf16[64,10,5760]{2,1,0:T(8,128)(2,1)}, u32[]{:S(2)}, u32[]{:S(2)}) async-start(bf16[64,10,5760]{2,1,0:T(8,128)(2,1)} %stack.6), calls=%async_computation | async-start | bytes 23592960 | tf_op jit(solution)/shard_map/all_to_all | solution.py:33
  24.4 20.6 %reshape.232 = f32[4,256,32,20]{3,2,1,0:T(8,128)} reshape(bf16[1,4,16,16,640]{4,3,2,1,0:T(8,128)(2,1)S(1)} %copy-done) | data formatting | bytes 3932160 | tf_op jit(solution)/shard_map/convert_element_type | solution.py:35
  46.6 11.4 %copy.33 = f32[4,256,32,20]{1,0,3,2:T(4,128)} copy(f32[4,256,32,20]{3,2,1,0:T(8,128)} %reshape.232) | data formatting | bytes 5242880 | tf_op jit(solution)/shard_map/convert_element_type | solution.py:35
  58.2 8.5 pad_slice_fusion.8
  66.7 108.5 %all-to-all-done = bf16[64,10,5760]{2,1,0:T(8,128)(2,1)} async-done(((bf16[64,10,5760]{2,1,0:T(8,128)(2,1)}), bf16[64,10,5760]{2,1,0:T(8,128)(2,1)}, u32[]{:S(2)}, u32[]{:S(2)}) %all-to-all-start) | async-done | bytes 7372832 | tf_op jit(solution)/shard_map/all_to_all | solution.py:33
  175.2 13.8 %reshape.211 = bf16[640,5760]{1,0:T(8,128)(2,1)} reshape(bf16[64,10,5760]{2,1,0:T(8,128)(2,1)} %all-to-all-done) | data formatting | bytes 14745600 | tf_op jit(solution)/shard_map/reshape | solution.py:32
  189.1 3.0 fusion.4
  199.8 2.8 fusion.18
  202.6 2.8 fusion.16
  205.5 6.2 fusion.28
  211.6 3.2 copy.31
  214.9 4.2 reshape.221
  219.1 16.5 %fusion.29 = (f32[4,32]{0,1:T(8,128)S(1)}, f32[4,32]{0,1:T(8,128)S(1)}) fusion(f32[4,32]{0,1:T(8,128)S(1)} %copy.34, f32[4,256,32,20]{1,0,3,2:T(4,128)} %copy.33, f32[4,32]{0,1:T(8,128)S(1)} %copy.32, f32[4,256,32,20]{1,0,3,2:T(4,128)} %reshape.221, f32[32,20]{1,0:T(8,128)S(1)} %add.134, f32[32,20]{1,0:T(8,128)S(1)} %mul.201), kind=kLoop, calls=%fused_computation.88 | loop fusion | flops 10485504 | bytes 5250048 | tf_op jit(solution)/shard_map/reduce_sum | solution.py:84
  236.1 3.6 multiply_convert_fusion
  239.7 3.0 pad_slice_fusion
  269.9 23.5 %collective-permute-start.1 = (bf16[1,80,256]{2,1,0:T(8,128)(2,1)S(1)}, bf16[1,80,256]{2,1,0:T(8,128)(2,1)S(1)}, u32[]{:S(2)}, u32[]{:S(2)}) collective-permute-start(bf16[1,80,256]{2,1,0:T(8,128)(2,1)S(1)} %fusion.2), channel_id=1, source_target_pairs={{0,2},{2,4},{4,6},{6,8},{8,10},{10,12},{12,14},{14,16},{16,18},{18... | collective-permute-start | bytes 122888 | tf_op jit(solution)/shard_map/ppermute | solution.py:17
  293.4 69.7 %all-reduce.3 = (f32[640]{0:T(1024)S(1)}, f32[640]{0:T(1024)S(1)}) all-reduce(f32[640]{0:T(1024)S(1)} %get-tuple-element.25, f32[640]{0:T(1024)S(1)} %get-tuple-element.24), channel_id=1, replica_groups=mesh['frames'=64,'dp'=2] {'frames','dp'}, use_global_device_ids=true, to_apply=%region_11.12 | all-reduce | flops 1280 | bytes 10240 | tf_op jit(solution)/shard_map/psum | solution.py:82
  367.2 518.1 %all-reduce.9.cloned.1.call-done = f32[640,5760]{0,1:T(8,128)} async-done(((f32[640,5760]{0,1:T(8,128)}), f32[640,5760]{0,1:T(8,128)}) %all-reduce.9.cloned.1.call-update) | async-done | bytes 14745616
  885.3 5.1 constant_dynamic-slice_fusion
  891.9 4.4 maximum_select_fusion
  896.3 82.4 %all-reduce.7.cloned.1.call-done = f32[10,5760]{0,1:T(8,128)} async-done(((f32[10,5760]{0,1:T(8,128)}), f32[10,5760]{0,1:T(8,128)}) %all-reduce.7.cloned.1.call-update) | async-done | bytes 230416 | tf_op jit(solution)/shard_map/psum | solution.py:76
  978.7 3.7 broadcast_multiply_fusion
  982.4 3.0 copy.37
  (88 shorter events, 42.1 us)
Async XLA Ops:
  13.1 11.3 %copy-start = (bf16[1,4,16,16,640]{4,3,2,1,0:T(8,128)(2,1)S(1)}, bf16[1,4,16,16,640]{4,3,2,1,0:T(8,128)(2,1)}, u32[]{:S(2)}) copy-start(bf16[1,4,16,16,640]{4,3,2,1,0:T(8,128)(2,1)} %param.7) | copy-start | bytes 3932164
  13.1 162.1 %all-to-all-start = ((bf16[64,10,5760]{2,1,0:T(8,128)(2,1)}), bf16[64,10,5760]{2,1,0:T(8,128)(2,1)}, u32[]{:S(2)}, u32[]{:S(2)}) async-start(bf16[64,10,5760]{2,1,0:T(8,128)(2,1)} %stack.6), calls=%async_computation | async-start | bytes 23592960 | tf_op jit(solution)/shard_map/all_to_all | solution.py:33
  24.4 861.0 %all-reduce.9.cloned.1.call-start = ((), (), s32[]{:S(2)}) async-start(), calls=%async_computation.2 | async-start | bytes 29491200
  46.6 11.4 %copy-start.12 = (f32[640]{0:T(1024)S(1)}, f32[640]{0:T(1024)}, u32[]{:S(2)}) copy-start(f32[640]{0:T(1024)} %param.11) | copy-start | bytes 7684
  46.6 11.5 %copy-start.13 = (f32[640]{0:T(1024)S(1)}, f32[640]{0:T(1024)}, u32[]{:S(2)}) copy-start(f32[640]{0:T(1024)} %param.10) | copy-start | bytes 7684
  189.1 3.7 copy-start.1
  189.1 4.0 copy-start.11
  193.1 1.3 copy-start.10
  194.5 1.3 copy-start.4
  195.8 1.3 copy-start.9
  197.1 1.3 copy-start.8
  198.5 1.3 copy-start.7
  199.8 2.8 copy-start.6
  239.7 3.0 copy-start.5
  264.6 0.7 copy-start.16
  264.6 1.9 copy-start.14
  264.6 1.9 copy-start.15
  264.6 714.1 %all-reduce.7.cloned.1.call-start = ((), (), s32[]{:S(2)}) async-start(), calls=%async_computation.1 | async-start | bytes 5898240 | tf_op jit(solution)/shard_map/psum | solution.py:76
  266.9 98.2 %collective-permute-start = (bf16[1,80,256]{2,1,0:T(8,128)(2,1)S(1)}, bf16[1,80,256]{2,1,0:T(8,128)(2,1)S(1)}, u32[]{:S(2)}, u32[]{:S(2)}) collective-permute-start(bf16[1,80,256]{2,1,0:T(8,128)(2,1)S(1)} %fusion.1), channel_id=1, source_target_pairs={{2,0},{4,2},{6,4},{8,6},{10,8},{12,10},{14,12},{16,14},{18,16},{20... | collective-permute-start | bytes 122888 | tf_op jit(solution)/shard_map/ppermute | solution.py:18
  269.9 96.2 %collective-permute-start.1 = (bf16[1,80,256]{2,1,0:T(8,128)(2,1)S(1)}, bf16[1,80,256]{2,1,0:T(8,128)(2,1)S(1)}, u32[]{:S(2)}, u32[]{:S(2)}) collective-permute-start(bf16[1,80,256]{2,1,0:T(8,128)(2,1)S(1)} %fusion.2), channel_id=1, source_target_pairs={{0,2},{2,4},{4,6},{6,8},{8,10},{10,12},{12,14},{14,16},{16,18},{18... | collective-permute-start | bytes 122888 | tf_op jit(solution)/shard_map/ppermute | solution.py:17
  890.4 1.2 copy-start.2
  890.4 1.5 copy-start.3
Sparse Core Ops, SparseCore 0:
  264.7 620.5 all-reduce.8
  890.5 88.0 all-reduce.6
